TPU v7x, 1024 devices: a whole 4x8x16 slice. The times are simulated.
1024 devices in a mesh: space: 64 (over z, y_hi), src: 16 (over x, y_lo, core).
Axes of the slice: x: 4, y: 8 (y_hi: 4, y_lo: 2; y = y_hi * 2 + y_lo), z: 16, core: 2. Of those that a mesh axis runs over, the one named last changes fastest.
Arguments:
- misfit: float32 [128, 131072], P('src', 'space'), may hold values from -6 to 6
- electrode_node: int32 [131072], P('space'), may hold values from 0 to 2047
- forward_field: bfloat16 [128, 131072], P('src', 'space'), may hold values from -16 to 16
- diag_blocks: bfloat16 [64, 131072], P(None, 'space'), may hold values from -0.125 to 1.125
- precond: bfloat16 [64, 131072], P(None, 'space'), may hold values from -0.125 to 1.125
- off_blocks: bfloat16 [6, 64, 131072], P(None, None, 'space'), may hold values from -0.3125 to 0.3125
- off_index: int32 [2048, 6], P('space'), may hold values from 0 to 55, as said below
Outputs:
- adjoint: float32 [128, 131072], P('src', 'space')
- gradient: float32 [131072], P(('space', 'src'))
Inputs may be any that keep to these rules, and one draw needn't show every extreme that they name: off_index of block b of a partition lies within b to b + 24 and is never b + 12.
All inputs are finite; a program needn't handle non-finite values.
Results may differ from a plain program's by a relative error of at most 0.0034.
Values may be sent and summed in bfloat16 or wider, within the bound.
A program may use at most 32 MiB of HBM per device.

v0:
```python
import jax
import jax.numpy as jnp
from jax import lax
from jax.sharding import PartitionSpec as P


def padded(block, sides, width):
    for axis, dim in sides:
        count = lax.axis_size(axis)
        forward = [(i, i + 1) for i in range(count - 1)]
        backward = [(target, source) for source, target in forward]
        low = lax.ppermute(
            lax.slice_in_dim(block, block.shape[dim] - width, None, axis=dim), axis, forward
        )
        high = lax.ppermute(lax.slice_in_dim(block, 0, width, axis=dim), axis, backward)
        block = jnp.concatenate([low, block, high], axis=dim)
    return block


def shards(misfit, electrode_node, forward_field, diag_blocks, precond, off_blocks, off_index):
    sources = misfit.shape[0]
    width = diag_blocks.shape[0]
    blocks = diag_blocks.shape[1] // width
    terms_per = off_blocks.shape[0]
    rim = 3 * blocks // 8
    nodes = blocks * width
    diag_view = diag_blocks.reshape(width, blocks, width)
    cond_view = precond.reshape(width, blocks, width)
    off_view = off_blocks.reshape(terms_per, width, blocks, width)

    def block_apply(extended):
        ext_blocks = extended.reshape(sources, blocks + 2 * rim, width)
        own = ext_blocks[:, rim : rim + blocks]
        picked = ext_blocks[:, off_index]
        result = jnp.einsum("ibj,sbj->sbi", diag_view, own, preferred_element_type=jnp.float32)
        result = result + jnp.einsum(
            "kibj,sbkj->sbi", off_view, picked, preferred_element_type=jnp.float32
        )
        return result.reshape(sources, nodes)

    def smooth(residue):
        rounded = residue.astype(jnp.bfloat16).reshape(sources, blocks, width)
        result = jnp.einsum("ibj,sbj->sbi", cond_view, rounded, preferred_element_type=jnp.float32)
        return result.reshape(sources, nodes)

    rhs = jnp.zeros((sources, nodes), jnp.float32).at[:, electrode_node].add(misfit)
    lam = smooth(rhs)
    lam_half = lam.astype(jnp.bfloat16)
    stacked = padded(jnp.stack([lam_half, forward_field]), (("space", 2),), rim * width)
    lam_ext = stacked[0]
    field_ext = stacked[1]
    lam = lam + smooth(rhs - block_apply(lam_ext))
    lam_ext = padded(lam.astype(jnp.bfloat16), (("space", 1),), rim * width)
    lam = lam + smooth(rhs - block_apply(lam_ext))
    driven = block_apply(field_ext)
    terms = -jnp.sum(lam * driven, axis=0)
    total = lax.psum(terms, "src")
    share = nodes // lax.axis_size("src")
    gradient = lax.dynamic_slice_in_dim(total, lax.axis_index("src") * share, share)
    return (lam, gradient)


def solution(mesh):
    return jax.shard_map(
        shards,
        mesh=mesh,
        in_specs=(
            P("src", "space"),
            P("space"),
            P("src", "space"),
            P(None, "space"),
            P(None, "space"),
            P(None, None, "space"),
            P("space", None),
        ),
        out_specs=(P("src", "space"), P(("space", "src"))),
        check_vma=False,
    )
```

profile of v0, /device:TPU:16, one launch (start us, length us, event | category | flops | bytes accessed | tf_op | source)
XLA Modules:
  0.0 102.7 jit_solution(5751195837006722502)
XLA Ops:
  0.6 0.0 copy-start.7
  0.6 0.0 copy-start.10
  0.7 0.0 copy-start.11
  0.7 1.2 %copy.49 = f32[2048,8]{1,0:T(8,128)S(1)} copy(f32[2048,8]{0,1:T(8,128)} %bitcast.55) | data formatting | bytes 131072 | tf_op args[0]
  1.9 0.7 compare_select_fusion
  2.6 11.7 %scatter_custom_fusion = f32[8,2048]{0,1:T(8,128)S(1)} fusion(s32[2048]{0:T(1024)S(1)} %compare_select_fusion, f32[2048,8]{1,0:T(8,128)S(1)} %copy.49, f32[]{:T(128)} %constant.6.clone.1), kind=kCustom, calls=%fused_computation.26 | custom fusion | flops 16384 | bytes 65540 | tf_op jit(solution)/shard_map/scatter-add | solution.py:46
  14.3 0.0 copy-start
  14.3 0.1 convert_element_type.34
  14.4 0.0 copy-done.7
  14.4 0.5 reshape.52
  14.9 0.0 copy-start.2
  14.9 0.4 fusion.28
  15.4 0.1 convert_element_type.37
  15.5 0.0 copy-done.10
  15.5 5.7 %collective-permute-start = (bf16[2,8,768]{2,1,0:T(8,128)(2,1)S(1)}, bf16[2,8,768]{2,1,0:T(8,128)(2,1)S(1)}, u32[]{:S(2)}, u32[]{:S(2)}) collective-permute-start(bf16[2,8,768]{2,1,0:T(8,128)(2,1)S(1)} %get-tuple-element.4), channel_id=1, source_target_pairs={{0,16},{16,32},{32,48},{48,64},{64,80},{80,96},{96,112},{112,128},... | collective-permute-start | bytes 73736 | tf_op jit(solution)/shard_map/ppermute | solution.py:12
  21.3 10.5 %collective-permute-start.1 = (bf16[2,8,768]{2,1,0:T(8,128)(2,1)S(1)}, bf16[2,8,768]{2,1,0:T(8,128)(2,1)S(1)}, u32[]{:S(2)}, u32[]{:S(2)}) collective-permute-start(bf16[2,8,768]{2,1,0:T(8,128)(2,1)S(1)} %get-tuple-element.5), channel_id=1, source_target_pairs={{16,0},{32,16},{48,32},{64,48},{80,64},{96,80},{112,96},{128,112},... | collective-permute-start | bytes 73736 | tf_op jit(solution)/shard_map/ppermute | solution.py:15
  31.7 0.0 copy-done.11
  31.8 0.1 copy.55
  31.9 0.1 reshape.62
  32.0 0.0 copy-done
  32.0 0.0 copy-done.2
  32.0 4.6 %reshape.54 = bf16[6,64,32,64]{3,2,1,0:T(8,128)(2,1)S(1)} reshape(bf16[6,64,2048]{2,1,0:T(8,128)(2,1)} %param.12) | data formatting | bytes 3145728 | tf_op jit(solution)/shard_map/reshape | solution.py:29
  36.6 2.3 %reshape.53 = bf16[64,32,64]{2,1,0:T(8,128)(2,1)} reshape(bf16[64,2048]{1,0:T(8,128)(2,1)} %param.10) | data formatting | bytes 524288 | tf_op jit(solution)/shard_map/reshape | solution.py:27
  38.9 0.0 collective-permute-done
  38.9 0.0 collective-permute-done.1
  38.9 0.8 pad_maximum_fusion
  39.6 0.6 fusion.33
  40.3 0.1 reshape_squeeze.6
  40.4 1.5 %gather_fusion = bf16[192,8,64]{2,1,0:T(8,128)(2,1)} fusion(bf16[8,56,64]{2,0,1:T(8,128)(2,1)S(1)} %copy.53, s32[1024]{0:T(1024)S(1)} %pad_clamp_fusion), kind=kCustom, calls=%fused_computation | custom fusion | bytes 393984 | tf_op jit(solution)/shard_map/gather | solution.py:34
  41.9 0.0 copy-start.4
  41.9 2.6 %fusion.9 = f32[32,8,64]{2,1,0:T(8,128)S(1)} fusion(bf16[8,32,6,64]{3,0,2,1:T(8,128)(2,1)} %bitcast.47, bf16[6,64,32,64]{3,2,1,0:T(8,128)(2,1)S(1)} %reshape.54), kind=kOutput, calls=%fused_computation.18 | convolution fusion | flops 12582912 | bytes 1835008 | tf_op jit(solution)/shard_map/kibj,sbkj->sbi/dot_general | solution.py:36
  44.5 0.0 copy-done.4
  44.6 1.1 %fusion.8 = f32[8,32,64]{2,0,1:T(8,128)} fusion(f32[32,8,64]{2,1,0:T(8,128)S(1)} %fusion.9, bf16[64,32,64]{2,1,0:T(8,128)(2,1)S(1)} %copy-done.4, bf16[8,56,64]{2,1,0:T(8,128)(2,1)S(1)} %reshape_squeeze.6), kind=kOutput, calls=%fused_computation.15 | convolution fusion | flops 2113536 | bytes 450560 | tf_op jit(solution)/shard_map/ibj,sbj->sbi/dot_general | solution.py:35
  45.6 2.3 %copy.82 = f32[8,32,64]{0,2,1:T(8,128)} copy(f32[8,32,64]{2,0,1:T(8,128)} %fusion.8) | data formatting | bytes 131072 | tf_op jit(solution)/shard_map/reshape | solution.py:39
  47.9 1.6 %fusion.20 = bf16[8,2048]{0,1:T(8,128)(2,1)S(1)} fusion(f32[8,2048]{0,1:T(8,128)} %copy-done, f32[8,32,64]{0,2,1:T(8,128)} %copy.82), kind=kLoop, calls=%fused_computation.25 | loop fusion | flops 32768 | bytes 163840 | tf_op jit(solution)/shard_map/convert_element_type | solution.py:42
  49.5 1.5 %convolution_add_fusion.4 = f32[32,8,64]{2,1,0:T(8,128)S(1)} fusion(f32[32,8,64]{2,1,0:T(8,128)S(1)} %fusion.28, bf16[8,32,64]{0,2,1:T(8,128)(2,1)S(1)} %bitcast.50, bf16[64,32,64]{2,1,0:T(8,128)(2,1)} %copy-done.2), kind=kOutput, calls=%fused_computation.17 | convolution fusion | flops 2113536 | bytes 425984 | tf_op jit(solution)/shard_map/ibj,sbj->sbi/dot_general | solution.py:43
  51.0 0.1 convert_element_type.41
  51.2 0.6 fusion.34
  51.8 1.9 %collective-permute-start.2 = (bf16[8,768]{1,0:T(8,128)(2,1)}, bf16[8,768]{1,0:T(8,128)(2,1)S(1)}, u32[]{:S(2)}, u32[]{:S(2)}) collective-permute-start(bf16[8,768]{1,0:T(8,128)(2,1)} %get-tuple-element.6), channel_id=1, source_target_pairs={{0,16},{16,32},{32,48},{48,64},{64,80},{80,96},{96,112},{112,128},... | collective-permute-start | bytes 36872 | tf_op jit(solution)/shard_map/ppermute | solution.py:12
  53.7 5.0 %collective-permute-start.3 = (bf16[8,768]{1,0:T(8,128)(2,1)S(1)}, bf16[8,768]{1,0:T(8,128)(2,1)S(1)}, u32[]{:S(2)}, u32[]{:S(2)}) collective-permute-start(bf16[8,768]{1,0:T(8,128)(2,1)S(1)} %get-tuple-element.7), channel_id=1, source_target_pairs={{16,0},{32,16},{48,32},{64,48},{80,64},{96,80},{112,96},{128,112},... | collective-permute-start | bytes 36872 | tf_op jit(solution)/shard_map/ppermute | solution.py:15
  58.7 0.0 copy-done.8
  58.7 0.9 reshape_squeeze.7
  59.7 1.5 %gather_fusion.2 = bf16[192,8,64]{2,1,0:T(8,128)(2,1)} fusion(bf16[8,56,64]{2,0,1:T(8,128)(2,1)S(1)} %copy.72, s32[1024]{0:T(1024)S(1)} %pad_clamp_fusion), kind=kCustom, calls=%fused_computation.2 | custom fusion | bytes 393984 | tf_op jit(solution)/shard_map/gather | solution.py:34
  61.2 3.2 %fusion.15 = f32[32,8,64]{2,1,0:T(8,128)} fusion(bf16[8,32,6,64]{3,0,2,1:T(8,128)(2,1)} %bitcast.48, bf16[6,64,32,64]{3,2,1,0:T(8,128)(2,1)S(1)} %reshape.54), kind=kOutput, calls=%fused_computation.20 | convolution fusion | flops 12582912 | bytes 1835008 | tf_op jit(solution)/shard_map/kibj,sbkj->sbi/dot_general | solution.py:36
  64.4 0.0 collective-permute-done.2
  64.4 0.0 collective-permute-done.3
  64.4 0.0 copy-done.9
  64.5 0.8 reshape.57
  65.2 0.9 copy.63
  66.2 1.5 %gather_fusion.1 = bf16[192,8,64]{2,1,0:T(8,128)(2,1)} fusion(bf16[8,56,64]{2,0,1:T(8,128)(2,1)S(1)} %copy.63, s32[1024]{0:T(1024)S(1)} %pad_clamp_fusion), kind=kCustom, calls=%fused_computation.1 | custom fusion | bytes 393984 | tf_op jit(solution)/shard_map/gather | solution.py:34
  67.6 2.6 %fusion.12 = f32[32,8,64]{2,1,0:T(8,128)S(1)} fusion(bf16[8,32,6,64]{3,0,2,1:T(8,128)(2,1)} %bitcast.46, bf16[6,64,32,64]{3,2,1,0:T(8,128)(2,1)S(1)} %reshape.54), kind=kOutput, calls=%fused_computation.19 | convolution fusion | flops 12582912 | bytes 1835008 | tf_op jit(solution)/shard_map/kibj,sbkj->sbi/dot_general | solution.py:36
  70.3 0.0 copy-done.5
  70.3 0.0 copy-done.6
  70.3 0.4 fusion.7
  70.7 0.4 copy.83
  71.0 0.5 copy-done.1
  71.5 0.1 fusion.19
  71.6 0.0 copy-done.3
  71.7 0.4 convolution_add_fusion.3
  72.1 1.5 %fusion.18 = f32[32,64]{1,0:T(8,128)S(1)} fusion(f32[32,8,64]{2,1,0:T(8,128)S(1)} %convolution_add_fusion.3, f32[32,8,64]{2,1,0:T(8,128)} %fusion.15, bf16[64,32,64]{2,1,0:T(8,128)(2,1)} %reshape.53, bf16[8,56,64]{2,1,0:T(8,128)(2,1)S(1)} %reshape_squeeze.7), kind=kOutput, calls=%fused_computation.21 | convolution fusion | flops 2144256 | bytes 458752 | tf_op jit(solution)/shard_map/ibj,sbj->sbi/dot_general | solution.py:35
  73.6 0.1 neg.7
  73.6 27.7 %psum.7 = f32[2048]{0:T(1024)S(1)} all-reduce(f32[2048]{0:T(1024)S(1)} %neg.7), channel_id=1, replica_groups=mesh['space'=64,'src'=16] {'src'}, use_global_device_ids=true, to_apply=%region_2.0 | all-reduce | flops 2048 | bytes 16384 | tf_op jit(solution)/shard_map/psum | solution.py:57
  101.4 0.7 add.62
  102.1 0.6 dynamic_slice.3
  (18 shorter events, 0.2 us)
Async XLA Ops:
  0.6 13.7 %copy-start.7 = (bf16[64,2048]{1,0:T(8,128)(2,1)S(1)}, bf16[64,2048]{1,0:T(8,128)(2,1)}, u32[]{:S(2)}) copy-start(bf16[64,2048]{1,0:T(8,128)(2,1)} %param.11) | copy-start | bytes 786436
  0.6 14.9 %copy-start.10 = (bf16[8,2048]{1,0:T(8,128)(2,1)S(1)}, bf16[8,2048]{1,0:T(8,128)(2,1)}, u32[]{:S(2)}) copy-start(bf16[8,2048]{1,0:T(8,128)(2,1)} %param.9) | copy-start | bytes 98308
  0.7 31.1 %copy-start.11 = (s32[32,6]{0,1:T(8,128)S(1)}, s32[32,6]{0,1:T(8,128)}, u32[]{:S(2)}) copy-start(s32[32,6]{0,1:T(8,128)} %param.13) | copy-start | bytes 2308
  14.3 17.7 %copy-start = (f32[8,2048]{0,1:T(8,128)}, f32[8,2048]{0,1:T(8,128)S(1)}, u32[]{:S(2)}) copy-start(f32[8,2048]{0,1:T(8,128)S(1)} %scatter_custom_fusion) | copy-start | bytes 196612
  14.9 17.1 %copy-start.2 = (bf16[64,32,64]{2,1,0:T(8,128)(2,1)}, bf16[64,32,64]{2,1,0:T(8,128)(2,1)S(1)}, u32[]{:S(2)}) copy-start(bf16[64,32,64]{2,1,0:T(8,128)(2,1)S(1)} %reshape.52) | copy-start | bytes 786436
  15.5 23.3 %collective-permute-start = (bf16[2,8,768]{2,1,0:T(8,128)(2,1)S(1)}, bf16[2,8,768]{2,1,0:T(8,128)(2,1)S(1)}, u32[]{:S(2)}, u32[]{:S(2)}) collective-permute-start(bf16[2,8,768]{2,1,0:T(8,128)(2,1)S(1)} %get-tuple-element.4), channel_id=1, source_target_pairs={{0,16},{16,32},{32,48},{48,64},{64,80},{80,96},{96,112},{112,128},... | collective-permute-start | bytes 73736 | tf_op jit(solution)/shard_map/ppermute | solution.py:12
  21.3 17.6 %collective-permute-start.1 = (bf16[2,8,768]{2,1,0:T(8,128)(2,1)S(1)}, bf16[2,8,768]{2,1,0:T(8,128)(2,1)S(1)}, u32[]{:S(2)}, u32[]{:S(2)}) collective-permute-start(bf16[2,8,768]{2,1,0:T(8,128)(2,1)S(1)} %get-tuple-element.5), channel_id=1, source_target_pairs={{16,0},{32,16},{48,32},{64,48},{80,64},{96,80},{112,96},{128,112},... | collective-permute-start | bytes 73736 | tf_op jit(solution)/shard_map/ppermute | solution.py:15
  41.9 2.6 %copy-start.4 = (bf16[64,32,64]{2,1,0:T(8,128)(2,1)S(1)}, bf16[64,32,64]{2,1,0:T(8,128)(2,1)}, u32[]{:S(2)}) copy-start(bf16[64,32,64]{2,1,0:T(8,128)(2,1)} %reshape.53) | copy-start | bytes 786436
  51.2 7.5 %copy-start.8 = (bf16[8,2048]{1,0:T(8,128)(2,1)}, bf16[8,2048]{1,0:T(8,128)(2,1)S(1)}, u32[]{:S(2)}) copy-start(bf16[8,2048]{1,0:T(8,128)(2,1)S(1)} %convert_element_type.41) | copy-start | bytes 98308
  51.8 12.6 %collective-permute-start.2 = (bf16[8,768]{1,0:T(8,128)(2,1)}, bf16[8,768]{1,0:T(8,128)(2,1)S(1)}, u32[]{:S(2)}, u32[]{:S(2)}) collective-permute-start(bf16[8,768]{1,0:T(8,128)(2,1)} %get-tuple-element.6), channel_id=1, source_target_pairs={{0,16},{16,32},{32,48},{48,64},{64,80},{80,96},{96,112},{112,128},... | collective-permute-start | bytes 36872 | tf_op jit(solution)/shard_map/ppermute | solution.py:12
  53.7 10.7 %collective-permute-start.3 = (bf16[8,768]{1,0:T(8,128)(2,1)S(1)}, bf16[8,768]{1,0:T(8,128)(2,1)S(1)}, u32[]{:S(2)}, u32[]{:S(2)}) collective-permute-start(bf16[8,768]{1,0:T(8,128)(2,1)S(1)} %get-tuple-element.7), channel_id=1, source_target_pairs={{16,0},{32,16},{48,32},{64,48},{80,64},{96,80},{112,96},{128,112},... | collective-permute-start | bytes 36872 | tf_op jit(solution)/shard_map/ppermute | solution.py:15
  61.2 3.2 %copy-start.9 = (bf16[8,2048]{1,0:T(8,128)(2,1)S(1)}, bf16[8,2048]{1,0:T(8,128)(2,1)}, u32[]{:S(2)}) copy-start(bf16[8,2048]{1,0:T(8,128)(2,1)} %copy-done.8) | copy-start | bytes 98308
  67.6 2.6 %copy-start.5 = (bf16[64,32,64]{2,1,0:T(8,128)(2,1)S(1)}, bf16[64,32,64]{2,1,0:T(8,128)(2,1)}, u32[]{:S(2)}) copy-start(bf16[64,32,64]{2,1,0:T(8,128)(2,1)} %reshape.53) | copy-start | bytes 786436
  67.6 2.6 %copy-start.6 = (bf16[8,56,64]{2,1,0:T(8,128)(2,1)S(1)}, bf16[8,56,64]{2,1,0:T(8,128)(2,1)}, u32[]{:S(2)}) copy-start(bf16[8,56,64]{2,1,0:T(8,128)(2,1)} %reshape.57) | copy-start | bytes 172036
  70.3 1.2 %copy-start.1 = (f32[8,2048]{0,1:T(8,128)S(1)}, f32[8,2048]{0,1:T(8,128)}, u32[]{:S(2)}) copy-start(f32[8,2048]{0,1:T(8,128)} %copy-done) | copy-start | bytes 196612
  70.3 1.4 %copy-start.3 = (bf16[64,32,64]{2,1,0:T(8,128)(2,1)S(1)}, bf16[64,32,64]{2,1,0:T(8,128)(2,1)}, u32[]{:S(2)}) copy-start(bf16[64,32,64]{2,1,0:T(8,128)(2,1)} %copy-done.2) | copy-start | bytes 786436
where the time goes:
time: 103 us
  blocking collectives  27.7 us (27%)
  starting transfers between devices  23.1 us (22%)
  local copies, waits for them, and re-layouts  22.1 us (21%)
  other arithmetic  15.1 us (15%)
  matrix products  13.7 us (13%)
    psum x1, blocking collectives, shards(): total = lax.psum(terms, 'src')  27.7 us
    ppermute x2, starting transfers between devices, padded(): lax.ppermute(lax.slice_in_dim(block, 0, width, axis=dim), axis, backward)  15.5 us
    scatter-add x1, other arithmetic, shards(): jnp.zeros((sources, nodes), jnp.float32).at[:, electrode_node].add(misfit)  11.7 us
    dot_general x3, matrix products, block_apply(): jnp.einsum('kibj,sbkj->sbi', off_view, picked, preferred_element_type=jnp...  8.5 us
    ppermute x2, starting transfers between devices, padded(): lax.ppermute(lax.slice_in_dim(block, block.shape[dim] - width, None, axis...  7.62 us
    reshape x1, local copies, waits for them, and re-layouts, shards(): off_view = off_blocks.reshape(terms_per, width, blocks, width)  4.58 us
    gather x3, local copies, waits for them, and re-layouts, block_apply(): picked = ext_blocks[:, off_index]  4.47 us
    dot_general x3, matrix products, block_apply(): jnp.einsum('ibj,sbj->sbi', diag_view, own, preferred_element_type=jnp.flo...  2.92 us
  transfers between devices with their start and end apart: 4, of which 0 were waited for; matrix products, arithmetic and copies ran while one was open for 12% of the time, Pallas kernels for 0%

commit v1 on v0

v1 whole, which is shorter than its diff:
```python
import functools

import jax
import jax.numpy as jnp
from jax import lax
from jax.experimental import pallas as pl
from jax.experimental.pallas import tpu as pltpu
from jax.sharding import PartitionSpec as P

MESH = pl.DeviceIdType.MESH
F32 = jnp.float32
BF16 = jnp.bfloat16
NT = (((1,), (1,)), ((), ()))


def kernel(
    cfg,
    misfit_h, node_h, field_h, diag_h, cond_h, off_h, index_h,
    lam_out, grad_out,
    misfit_v, node_v, field_v, diag_v, cond_v, off_v, index_s,
    rhs_v, lam_v, driven_v, tiles1, tiles2, tiles_f,
    stage, landed, grad_send, grad_recv,
    load_sem, halo_send, halo_recv, gsend_sem, grecv_sem,
):
    spaces, groups, pairs, rim, terms = cfg
    blocks = 2 * pairs
    ext = rim // 2
    inner = range(ext, pairs - ext)
    low = range(0, ext)
    high = range(pairs - ext, pairs)

    loads = []
    for at, (src, dst) in enumerate(
        [
            (node_h, node_v), (misfit_h, misfit_v), (cond_h, cond_v), (field_h, field_v),
            (index_h, index_s), (diag_h, diag_v), (off_h, off_v),
        ]
    ):
        copy = pltpu.make_async_copy(src, dst, load_sem.at[at])
        copy.start()
        loads.append(copy)
    node_l, misfit_l, cond_l, field_l, index_l, diag_l, off_l = loads

    me = lax.axis_index("space")
    group = lax.axis_index("src")
    down = lax.rem(me + spaces - 1, spaces)
    up = lax.rem(me + 1, spaces)
    barrier = pltpu.get_barrier_semaphore()
    for neighbour in (down, up):
        pl.semaphore_signal(barrier, inc=1, device_id={"space": neighbour}, device_id_type=MESH)
    for step in range(1, groups):
        peer = lax.rem(group + step, groups)
        pl.semaphore_signal(barrier, inc=1, device_id={"src": peer}, device_id_type=MESH)

    left = lax.broadcasted_iota(jnp.int32, (8, 128), 1) < 64
    upper_rows = lax.broadcasted_iota(jnp.int32, (16, 128), 0) < 8
    zero = jnp.zeros((8, 128), F32)

    def lanes(pair):
        return pl.ds(pair * 128, 128)

    node_l.wait()
    misfit_l.wait()
    chunk = 256
    total = None
    for at in range(0, misfit_v.shape[1], chunk):
        node = node_v[:, pl.ds(at, chunk)]
        pair_of = jnp.broadcast_to(node // 128, (8, chunk))
        lane_of = jnp.broadcast_to(node % 128, (128, chunk))
        value = misfit_v[:, pl.ds(at, chunk)]
        coarse = value.astype(BF16).astype(F32)
        fine = value - coarse
        rows = []
        for pair in range(pairs):
            mask = pair_of == pair
            rows.append(jnp.where(mask, coarse, 0.0))
            rows.append(jnp.where(mask, fine, 0.0))
        spread = jnp.concatenate(rows, axis=0).astype(BF16)
        hot = lax.broadcasted_iota(jnp.int32, (128, chunk), 0) == lane_of
        hot = jnp.where(hot, 1.0, 0.0).astype(BF16)
        part = lax.dot_general(spread, hot, NT, preferred_element_type=F32)
        total = part if total is None else total + part
    rhs = [total[16 * p : 16 * p + 8] + total[16 * p + 8 : 16 * p + 16] for p in range(pairs)]
    for pair in range(pairs):
        rhs_v[pair] = rhs[pair]

    def join(y):
        return jnp.where(left, y[0:8], y[8:16])

    def smooth(pair, res):
        x = jnp.concatenate([jnp.where(left, res, zero), jnp.where(left, zero, res)], axis=0)
        w = cond_v[:, lanes(pair)]
        w = jnp.concatenate([w, w], axis=0)
        return join(lax.dot_general(x.astype(BF16), w, NT, preferred_element_type=F32))

    def expand(tiles, first, v):
        swapped = pltpu.roll(v, 64, 1)
        tiles[first] = jnp.concatenate(
            [jnp.where(left, v, zero), jnp.where(left, zero, swapped)], axis=0
        ).astype(BF16)
        tiles[first + 1] = jnp.concatenate(
            [jnp.where(left, swapped, zero), jnp.where(left, zero, v)], axis=0
        ).astype(BF16)

    def apply(pair, tiles):
        parts = [jnp.where(upper_rows, tiles[rim + 2 * pair], tiles[rim + 2 * pair + 1])]
        weights = [diag_v[:, lanes(pair)]]
        for k in range(terms):
            parts.append(
                jnp.where(
                    upper_rows,
                    tiles[index_s[k, 2 * pair]],
                    tiles[index_s[k, 2 * pair + 1]],
                )
            )
            weights.append(off_v[k, :, lanes(pair)])
        x = jnp.concatenate(parts, axis=1)
        w = jnp.concatenate(weights, axis=1)
        w = jnp.concatenate([w, w], axis=0)
        return join(lax.dot_general(x, w, NT, preferred_element_type=F32))

    def stage_side(which, side, values):
        for at in range(0, ext, 2):
            stage[which, side, at // 2] = jnp.concatenate(
                [values[at], values[at + 1]], axis=0
            ).astype(BF16)

    def halo(which, side):
        return pltpu.make_async_remote_copy(
            src_ref=stage.at[which, side],
            dst_ref=landed.at[which, 1 - side],
            send_sem=halo_send.at[2 * which + side],
            recv_sem=halo_recv.at[2 * which + 1 - side],
            device_id={"space": down if side == 0 else up},
            device_id_type=MESH,
        )

    def receive(which, side, tiles):
        halo(which, 1 - side).wait_recv()
        have = me > 0 if side == 0 else me < spaces - 1
        base = 0 if side == 0 else rim + blocks
        for at in range(0, ext, 2):
            both = landed[which, side, at // 2].astype(F32)
            both = jnp.where(have, both, 0.0)
            expand(tiles, base + 2 * at, both[0:8])
            expand(tiles, base + 2 * at + 2, both[8:16])

    cond_l.wait()
    lam = [None] * pairs
    for pair in (*low, *high):
        lam[pair] = smooth(pair, rhs[pair])
    stage_side(0, 0, [lam[p] for p in low])
    stage_side(0, 1, [lam[p] for p in high])
    field_l.wait()
    field = [field_v[:, lanes(p)].astype(F32) for p in range(pairs)]
    stage_side(2, 0, [field[p] for p in low])
    stage_side(2, 1, [field[p] for p in high])

    pl.semaphore_wait(barrier, groups + 1)
    for which in (0, 2):
        for side in (0, 1):
            halo(which, side).start()

    for pair in inner:
        lam[pair] = smooth(pair, rhs[pair])
    for pair in range(pairs):
        lam_v[pair] = lam[pair]
        expand(tiles1, rim + 2 * pair, lam[pair])
        expand(tiles_f, rim + 2 * pair, field[pair])

    index_l.wait()
    diag_l.wait()
    off_l.wait()

    def sweep(pair, tiles):
        new = lam_v[pair] + smooth(pair, rhs_v[pair] - apply(pair, tiles))
        lam_v[pair] = new
        return new

    for pair in inner:
        lam[pair] = sweep(pair, tiles1)
    for side, own in ((0, low), (1, high)):
        receive(0, side, tiles1)
        for pair in own:
            lam[pair] = sweep(pair, tiles1)
        stage_side(1, side, [lam[p] for p in own])
        halo(1, side).start()
    for pair in range(pairs):
        expand(tiles2, rim + 2 * pair, lam[pair])

    for side in (0, 1):
        receive(2, side, tiles_f)
    for pair in range(pairs):
        driven_v[pair] = apply(pair, tiles_f)

    def send_row(pair):
        return pltpu.make_async_remote_copy(
            src_ref=grad_send.at[pair],
            dst_ref=grad_recv.at[group],
            send_sem=gsend_sem.at[pair],
            recv_sem=grecv_sem.at[group],
            device_id={"src": pair},
            device_id_type=MESH,
        )

    def finish(pair):
        new = sweep(pair, tiles2)
        lam_out[:, lanes(pair)] = new
        row = -jnp.sum(new * driven_v[pair], axis=0, keepdims=True)
        grad_send[pair] = row

        @pl.when(group != pair)
        def _():
            send_row(pair).start()

        @pl.when(group == pair)
        def _():
            grad_recv[pair] = row

    for pair in inner:
        finish(pair)
    for side, own in ((0, low), (1, high)):
        receive(1, side, tiles2)
        for pair in own:
            finish(pair)

    for which in range(3):
        for side in (0, 1):
            halo(which, side).wait_send()
    for peer in range(groups):

        @pl.when(group != peer)
        def _():
            pltpu.make_async_remote_copy(
                src_ref=grad_send.at[peer],
                dst_ref=grad_recv.at[peer],
                send_sem=gsend_sem.at[peer],
                recv_sem=grecv_sem.at[peer],
                device_id={"src": peer},
                device_id_type=MESH,
            ).wait()

    grad_out[...] = jnp.sum(grad_recv[...], axis=0)


def solution(mesh):
    spaces, groups = mesh.shape["space"], mesh.shape["src"]

    def shards(misfit, electrode_node, forward_field, diag_blocks, precond, off_blocks, off_index):
        sources, nodes = forward_field.shape
        width = diag_blocks.shape[0]
        blocks = nodes // width
        terms = off_blocks.shape[0]
        rim = 3 * blocks // 8
        pairs = blocks // 2
        electrodes = misfit.shape[1]
        ext_blocks = blocks + 2 * rim
        sent = rim // 4
        lam, grad = pl.pallas_call(
            functools.partial(kernel, (spaces, groups, pairs, rim, terms)),
            out_shape=(
                jax.ShapeDtypeStruct((sources, nodes), F32),
                jax.ShapeDtypeStruct((1, nodes // groups), F32),
            ),
            in_specs=[pl.BlockSpec(memory_space=pl.ANY)] * 7,
            out_specs=(pl.BlockSpec(memory_space=pltpu.VMEM), pl.BlockSpec(memory_space=pltpu.VMEM)),
            scratch_shapes=[
                pltpu.VMEM((sources, electrodes), F32),
                pltpu.VMEM((1, electrodes), jnp.int32),
                pltpu.VMEM((sources, nodes), BF16),
                pltpu.VMEM((width, nodes), BF16),
                pltpu.VMEM((width, nodes), BF16),
                pltpu.VMEM((terms, width, nodes), BF16),
                pltpu.SMEM((terms, blocks), jnp.int32),
                pltpu.VMEM((pairs, sources, 128), F32),
                pltpu.VMEM((pairs, sources, 128), F32),
                pltpu.VMEM((pairs, sources, 128), F32),
                pltpu.VMEM((ext_blocks, 16, 128), BF16),
                pltpu.VMEM((ext_blocks, 16, 128), BF16),
                pltpu.VMEM((ext_blocks, 16, 128), BF16),
                pltpu.VMEM((3, 2, sent, 16, 128), BF16),
                pltpu.VMEM((3, 2, sent, 16, 128), BF16),
                pltpu.VMEM((pairs, 1, 128), F32),
                pltpu.VMEM((groups, 1, 128), F32),
                pltpu.SemaphoreType.DMA((7,)),
                pltpu.SemaphoreType.DMA((6,)),
                pltpu.SemaphoreType.DMA((6,)),
                pltpu.SemaphoreType.DMA((pairs,)),
                pltpu.SemaphoreType.DMA((groups,)),
            ],
            compiler_params=pltpu.CompilerParams(
                collective_id=0, has_side_effects=True, vmem_limit_bytes=48 * 1024 * 1024
            ),
        )(
            misfit, electrode_node.reshape(1, electrodes), forward_field, diag_blocks, precond,
            off_blocks, off_index.T,
        )
        return lam, grad.reshape(nodes // groups)

    return jax.shard_map(
        shards,
        mesh=mesh,
        in_specs=(
            P("src", "space"),
            P("space"),
            P("src", "space"),
            P(None, "space"),
            P(None, "space"),
            P(None, None, "space"),
            P("space", None),
        ),
        out_specs=(P("src", "space"), P(("space", "src"))),
        check_vma=False,
    )
```

time: 103 us -> 49.2 us (0.48)
  the two profiles are of different devices: /device:TPU:16 before, /device:TPU:6 now
where the time goes in v1:
time: 49.2 us; the launch traced here: 48.4 us
  Pallas kernels  40.3 us (82%)
  local copies, waits for them, and re-layouts  7.42 us (15%)
  between operations  0.66 us (1%)
    pallas_call x1, Pallas kernels, shards(): pl.pallas_call(functools.partial(kernel, (spaces, groups, pairs, rim, ter...  40.3 us
    unnamed x16, local copies, waits for them, and re-layouts  7.42 us

profile of v1, /device:TPU:6, one launch (start us, length us, event | category | flops | bytes accessed | tf_op | source)
XLA Modules:
  0.0 48.4 jit_solution(8200925089486125585)
XLA Ops:
  0.6 0.0 copy-start
  0.6 1.4 %copy-done = bf16[6,64,2048]{2,1,0:T(8,128)(2,1)S(1)} copy-done((bf16[6,64,2048]{2,1,0:T(8,128)(2,1)S(1)}, bf16[6,64,2048]{2,1,0:T(8,128)(2,1)}, u32[]{:S(2)}) %copy-start) | copy-done | bytes 1572888
  2.0 0.0 copy-start.1
  2.0 0.9 %copy-done.1 = bf16[64,2048]{1,0:T(8,128)(2,1)S(1)} copy-done((bf16[64,2048]{1,0:T(8,128)(2,1)S(1)}, bf16[64,2048]{1,0:T(8,128)(2,1)}, u32[]{:S(2)}) %copy-start.1) | copy-done | bytes 262168
  3.0 0.0 copy-start.2
  3.0 0.9 %copy-done.2 = bf16[64,2048]{1,0:T(8,128)(2,1)S(1)} copy-done((bf16[64,2048]{1,0:T(8,128)(2,1)S(1)}, bf16[64,2048]{1,0:T(8,128)(2,1)}, u32[]{:S(2)}) %copy-start.2) | copy-done | bytes 262168
  3.9 0.0 copy-start.3
  3.9 0.8 %copy-done.3 = f32[8,2048]{1,0:T(8,128)S(1)} copy-done((f32[8,2048]{1,0:T(8,128)S(1)}, f32[8,2048]{1,0:T(8,128)}, u32[]{:S(2)}) %copy-start.3) | copy-done | bytes 65560
  4.8 0.0 copy-start.4
  4.8 0.8 %copy-done.4 = bf16[8,2048]{1,0:T(8,128)(2,1)S(1)} copy-done((bf16[8,2048]{1,0:T(8,128)(2,1)S(1)}, bf16[8,2048]{1,0:T(8,128)(2,1)}, u32[]{:S(2)}) %copy-start.4) | copy-done | bytes 32792
  5.5 0.0 copy-start.5
  5.5 0.7 %copy-done.5 = s32[2048]{0:T(1024)S(1)} copy-done((s32[2048]{0:T(1024)S(1)}, s32[2048]{0:T(1024)}, u32[]{:S(2)}) %copy-start.5) | copy-done | bytes 8216
  6.2 0.0 copy-start.6
  6.2 0.7 %copy-done.6 = s32[32,6]{0,1:T(8,128)S(1)} copy-done((s32[32,6]{0,1:T(8,128)S(1)}, s32[32,6]{0,1:T(8,128)}, u32[]{:S(2)}) %copy-start.6) | copy-done | bytes 792
  6.9 40.3 %shard_map.86 = (f32[8,2048]{1,0:T(8,128)S(1)}, f32[1,128]{1,0:T(1,128)S(1)}) custom-call(f32[8,2048]{1,0:T(8,128)S(1)} %copy-done.3, s32[1,2048]{1,0:T(1,128)S(1)} %bitcast.3, bf16[8,2048]{1,0:T(8,128)(2,1)S(1)} %copy-done.4, bf16[64,2048]{1,0:T(8,128)(2,1)S(1)} %copy-done.1, bf16[64,2048]{1,0:T(8,128)(2,1)S(1)} %copy-done.2, ...), custom_call_target="tpu_custom_call" | custom-call | tf_op jit(solution)/shard_map/pallas_call | solution.py:259
  47.2 0.6 %copy.11 = f32[8,2048]{1,0:T(8,128)} copy(f32[8,2048]{1,0:T(8,128)S(1)} %get-tuple-element.8) | data formatting | bytes 131072
  47.9 0.5 %copy.12 = f32[128]{0:T(128)} copy(f32[128]{0:T(128)S(1)} %bitcast.5) | data formatting | bytes 1024
Async XLA Ops:
  0.6 1.4 %copy-start = (bf16[6,64,2048]{2,1,0:T(8,128)(2,1)S(1)}, bf16[6,64,2048]{2,1,0:T(8,128)(2,1)}, u32[]{:S(2)}) copy-start(bf16[6,64,2048]{2,1,0:T(8,128)(2,1)} %off_h.1) | copy-start | bytes 4718596
  2.0 0.9 %copy-start.1 = (bf16[64,2048]{1,0:T(8,128)(2,1)S(1)}, bf16[64,2048]{1,0:T(8,128)(2,1)}, u32[]{:S(2)}) copy-start(bf16[64,2048]{1,0:T(8,128)(2,1)} %diag_h.1) | copy-start | bytes 786436
  3.0 0.9 %copy-start.2 = (bf16[64,2048]{1,0:T(8,128)(2,1)S(1)}, bf16[64,2048]{1,0:T(8,128)(2,1)}, u32[]{:S(2)}) copy-start(bf16[64,2048]{1,0:T(8,128)(2,1)} %cond_h.1) | copy-start | bytes 786436
  3.9 0.8 %copy-start.3 = (f32[8,2048]{1,0:T(8,128)S(1)}, f32[8,2048]{1,0:T(8,128)}, u32[]{:S(2)}) copy-start(f32[8,2048]{1,0:T(8,128)} %misfit_h.1) | copy-start | bytes 196612
  4.8 0.8 %copy-start.4 = (bf16[8,2048]{1,0:T(8,128)(2,1)S(1)}, bf16[8,2048]{1,0:T(8,128)(2,1)}, u32[]{:S(2)}) copy-start(bf16[8,2048]{1,0:T(8,128)(2,1)} %field_h.1) | copy-start | bytes 98308
  5.5 0.7 %copy-start.5 = (s32[2048]{0:T(1024)S(1)}, s32[2048]{0:T(1024)}, u32[]{:S(2)}) copy-start(s32[2048]{0:T(1024)} %param.8) | copy-start | bytes 24580
  6.2 0.7 %copy-start.6 = (s32[32,6]{0,1:T(8,128)S(1)}, s32[32,6]{0,1:T(8,128)}, u32[]{:S(2)}) copy-start(s32[32,6]{0,1:T(8,128)} %param.13) | copy-start | bytes 2308

commit v2 on v1

--- a/solution.py
+++ b/solution.py
@@ -18,7 +18,7 @@
     misfit_h, node_h, field_h, diag_h, cond_h, off_h, index_h,
     lam_out, grad_out,
     misfit_v, node_v, field_v, diag_v, cond_v, off_v, index_s,
-    rhs_v, lam_v, driven_v, tiles1, tiles2, tiles_f,
+    rhs_v, driven_v, tiles1, tiles2, tiles_f,
     stage, landed, grad_send, grad_recv,
     load_sem, halo_send, halo_recv, gsend_sem, grecv_sem,
 ):
@@ -164,7 +164,6 @@
     for pair in inner:
         lam[pair] = smooth(pair, rhs[pair])
     for pair in range(pairs):
-        lam_v[pair] = lam[pair]
         expand(tiles1, rim + 2 * pair, lam[pair])
         expand(tiles_f, rim + 2 * pair, field[pair])
 
@@ -172,17 +171,16 @@
     diag_l.wait()
     off_l.wait()
 
-    def sweep(pair, tiles):
-        new = lam_v[pair] + smooth(pair, rhs_v[pair] - apply(pair, tiles))
-        lam_v[pair] = new
-        return new
-
-    for pair in inner:
-        lam[pair] = sweep(pair, tiles1)
+    def sweep(some, tiles):
+        products = [apply(pair, tiles) for pair in some]
+        steps = [smooth(pair, rhs_v[pair] - y) for pair, y in zip(some, products)]
+        for pair, step in zip(some, steps):
+            lam[pair] = lam[pair] + step
+
+    sweep(inner, tiles1)
     for side, own in ((0, low), (1, high)):
         receive(0, side, tiles1)
-        for pair in own:
-            lam[pair] = sweep(pair, tiles1)
+        sweep(own, tiles1)
         stage_side(1, side, [lam[p] for p in own])
         halo(1, side).start()
     for pair in range(pairs):
@@ -203,27 +201,24 @@
             device_id_type=MESH,
         )
 
-    def finish(pair):
-        new = sweep(pair, tiles2)
-        lam_out[:, lanes(pair)] = new
-        row = -jnp.sum(new * driven_v[pair], axis=0, keepdims=True)
-        grad_send[pair] = row
-
-        @pl.when(group != pair)
-        def _():
-            send_row(pair).start()
-
-        @pl.when(group == pair)
-        def _():
-            grad_recv[pair] = row
-
-    for pair in inner:
-        finish(pair)
+    def finish(some):
+        sweep(some, tiles2)
+        rows = [-jnp.sum(lam[p] * driven_v[p], axis=0, keepdims=True) for p in some]
+        for pair, row in zip(some, rows):
+            grad_send[pair] = row
+            lam_out[:, lanes(pair)] = lam[pair]
+        for pair in some:
+
+            @pl.when(group != pair)
+            def _():
+                send_row(pair).start()
+
+    finish(inner)
     for side, own in ((0, low), (1, high)):
         receive(1, side, tiles2)
-        for pair in own:
-            finish(pair)
-
+        finish(own)
+
+    grad_recv[pl.ds(group, 1)] = grad_send[pl.ds(group, 1)]
     for which in range(3):
         for side in (0, 1):
             halo(which, side).wait_send()
@@ -262,7 +257,7 @@
                 jax.ShapeDtypeStruct((sources, nodes), F32),
                 jax.ShapeDtypeStruct((1, nodes // groups), F32),
             ),
-            in_specs=[pl.BlockSpec(memory_space=pl.ANY)] * 7,
+            in_specs=[pl.BlockSpec(memory_space=pltpu.HBM)] * 7,
             out_specs=(pl.BlockSpec(memory_space=pltpu.VMEM), pl.BlockSpec(memory_space=pltpu.VMEM)),
             scratch_shapes=[
                 pltpu.VMEM((sources, electrodes), F32),
@@ -272,7 +267,6 @@
                 pltpu.VMEM((width, nodes), BF16),
                 pltpu.VMEM((terms, width, nodes), BF16),
                 pltpu.SMEM((terms, blocks), jnp.int32),
-                pltpu.VMEM((pairs, sources, 128), F32),
                 pltpu.VMEM((pairs, sources, 128), F32),
                 pltpu.VMEM((pairs, sources, 128), F32),
                 pltpu.VMEM((ext_blocks, 16, 128), BF16),
@@ -289,7 +283,7 @@
                 pltpu.SemaphoreType.DMA((groups,)),
             ],
             compiler_params=pltpu.CompilerParams(
-                collective_id=0, has_side_effects=True, vmem_limit_bytes=48 * 1024 * 1024
+                collective_id=0, has_side_effects=True, vmem_limit_bytes=60 * 1024 * 1024
             ),
         )(
             misfit, electrode_node.reshape(1, electrodes), forward_field, diag_blocks, precond,

time: 49.2 us -> 41.9 us (0.85)
  the two profiles are of different devices: /device:TPU:6 before, /device:TPU:1 now
where the time goes in v2:
time: 41.9 us; the launch traced here: 41.7 us
  Pallas kernels  38.4 us (92%)
  local copies, waits for them, and re-layouts  2.59 us (6%)
  between operations  0.64 us (2%)
    pallas_call x1, Pallas kernels, shards(): pl.pallas_call(functools.partial(kernel, (spaces, groups, pairs, rim, ter...  38.4 us
    unnamed x2, local copies, waits for them, and re-layouts  2.59 us

profile of v2, /device:TPU:1, one launch (start us, length us, event | category | flops | bytes accessed | tf_op | source)
XLA Modules:
  0.0 41.7 jit_solution(5156129040336778375)
XLA Ops:
  0.6 38.4 %shard_map.86 = (f32[8,2048]{1,0:T(8,128)}, f32[1,128]{1,0:T(1,128)}) custom-call(f32[8,2048]{1,0:T(8,128)} %misfit_h.1, s32[1,2048]{1,0:T(1,128)} %bitcast.3, bf16[8,2048]{1,0:T(8,128)(2,1)} %field_h.1, bf16[64,2048]{1,0:T(8,128)(2,1)} %diag_h.1, bf16[64,2048]{1,0:T(8,128)(2,1)} %cond_h.1, bf16[6,64,2048]{2,1,0:T(8,128)(2,1)} %off_h.1, s32[6,32]{1,0:T(8,128)} %bitcast.4), custom_call_target="tpu_custom_call" | custom-call | tf_op jit(solution)/shard_map/pallas_call | solution.py:254
  39.1 1.5 %copy.11 = f32[8,2048]{1,0:T(8,128)} copy(f32[8,2048]{1,0:T(8,128)} %get-tuple-element.8) | data formatting | bytes 131072
  40.6 1.1 %copy.12 = f32[128]{0:T(128)} copy(f32[128]{0:T(128)} %bitcast.5) | data formatting | bytes 1024

commit v3 on v2

--- a/solution.py
+++ b/solution.py
@@ -46,8 +46,15 @@
     down = lax.rem(me + spaces - 1, spaces)
     up = lax.rem(me + 1, spaces)
     barrier = pltpu.get_barrier_semaphore()
-    for neighbour in (down, up):
-        pl.semaphore_signal(barrier, inc=1, device_id={"space": neighbour}, device_id_type=MESH)
+    has = (me > 0, me < spaces - 1)
+    for side, neighbour in enumerate((down, up)):
+
+        @pl.when(has[side])
+        def _():
+            pl.semaphore_signal(
+                barrier, inc=1, device_id={"space": neighbour}, device_id_type=MESH
+            )
+
     for step in range(1, groups):
         peer = lax.rem(group + step, groups)
         pl.semaphore_signal(barrier, inc=1, device_id={"src": peer}, device_id_type=MESH)
@@ -85,12 +92,11 @@
         rhs_v[pair] = rhs[pair]
 
     def join(y):
-        return jnp.where(left, y[0:8], y[8:16])
+        return jnp.concatenate([y[0:8], y[8:16]], axis=1)
 
     def smooth(pair, res):
         x = jnp.concatenate([jnp.where(left, res, zero), jnp.where(left, zero, res)], axis=0)
         w = cond_v[:, lanes(pair)]
-        w = jnp.concatenate([w, w], axis=0)
         return join(lax.dot_general(x.astype(BF16), w, NT, preferred_element_type=F32))
 
     def expand(tiles, first, v):
@@ -116,7 +122,6 @@
             weights.append(off_v[k, :, lanes(pair)])
         x = jnp.concatenate(parts, axis=1)
         w = jnp.concatenate(weights, axis=1)
-        w = jnp.concatenate([w, w], axis=0)
         return join(lax.dot_general(x, w, NT, preferred_element_type=F32))
 
     def stage_side(which, side, values):
@@ -135,13 +140,20 @@
             device_id_type=MESH,
         )
 
+    def start(which, side):
+        @pl.when(has[side])
+        def _():
+            halo(which, side).start()
+
     def receive(which, side, tiles):
-        halo(which, 1 - side).wait_recv()
-        have = me > 0 if side == 0 else me < spaces - 1
+        @pl.when(has[side])
+        def _():
+            halo(which, 1 - side).wait_recv()
+
         base = 0 if side == 0 else rim + blocks
         for at in range(0, ext, 2):
             both = landed[which, side, at // 2].astype(F32)
-            both = jnp.where(have, both, 0.0)
+            both = jnp.where(has[side], both, 0.0)
             expand(tiles, base + 2 * at, both[0:8])
             expand(tiles, base + 2 * at + 2, both[8:16])
 
@@ -156,10 +168,12 @@
     stage_side(2, 0, [field[p] for p in low])
     stage_side(2, 1, [field[p] for p in high])
 
-    pl.semaphore_wait(barrier, groups + 1)
+    pl.semaphore_wait(
+        barrier, groups - 1 + jnp.where(has[0], 1, 0) + jnp.where(has[1], 1, 0)
+    )
     for which in (0, 2):
         for side in (0, 1):
-            halo(which, side).start()
+            start(which, side)
 
     for pair in inner:
         lam[pair] = smooth(pair, rhs[pair])
@@ -182,7 +196,7 @@
         receive(0, side, tiles1)
         sweep(own, tiles1)
         stage_side(1, side, [lam[p] for p in own])
-        halo(1, side).start()
+        start(1, side)
     for pair in range(pairs):
         expand(tiles2, rim + 2 * pair, lam[pair])
 
@@ -221,7 +235,11 @@
     grad_recv[pl.ds(group, 1)] = grad_send[pl.ds(group, 1)]
     for which in range(3):
         for side in (0, 1):
-            halo(which, side).wait_send()
+
+            @pl.when(has[side])
+            def _():
+                halo(which, side).wait_send()
+
     for peer in range(groups):
 
         @pl.when(group != peer)
@@ -236,6 +254,17 @@
             ).wait()
 
     grad_out[...] = jnp.sum(grad_recv[...], axis=0)
+
+
+def write_out(lam, grad, lam_out, grad_out, sem):
+    copies = [
+        pltpu.make_async_copy(lam, lam_out, sem.at[0]),
+        pltpu.make_async_copy(grad, grad_out, sem.at[1]),
+    ]
+    for copy in copies:
+        copy.start()
+    for copy in copies:
+        copy.wait()
 
 
 def solution(mesh):
@@ -254,8 +283,8 @@
         lam, grad = pl.pallas_call(
             functools.partial(kernel, (spaces, groups, pairs, rim, terms)),
             out_shape=(
-                jax.ShapeDtypeStruct((sources, nodes), F32),
-                jax.ShapeDtypeStruct((1, nodes // groups), F32),
+                pltpu.VMEM((sources, nodes), F32),
+                pltpu.VMEM((1, nodes // groups), F32),
             ),
             in_specs=[pl.BlockSpec(memory_space=pltpu.HBM)] * 7,
             out_specs=(pl.BlockSpec(memory_space=pltpu.VMEM), pl.BlockSpec(memory_space=pltpu.VMEM)),
@@ -283,11 +312,29 @@
                 pltpu.SemaphoreType.DMA((groups,)),
             ],
             compiler_params=pltpu.CompilerParams(
-                collective_id=0, has_side_effects=True, vmem_limit_bytes=60 * 1024 * 1024
+                collective_id=0, has_side_effects=True, vmem_limit_bytes=32 * 1024 * 1024
             ),
         )(
-            misfit, electrode_node.reshape(1, electrodes), forward_field, diag_blocks, precond,
-            off_blocks, off_index.T,
+            *(
+                pltpu.with_memory_space_constraint(operand, pltpu.HBM)
+                for operand in (
+                    misfit, electrode_node.reshape(1, electrodes), forward_field, diag_blocks,
+                    precond, off_blocks, off_index.T,
+                )
+            )
+        )
+        lam, grad = pl.pallas_call(
+            write_out,
+            out_shape=(
+                pltpu.HBM((sources, nodes), F32),
+                pltpu.HBM((1, nodes // groups), F32),
+            ),
+            in_specs=[pl.BlockSpec(memory_space=pltpu.VMEM)] * 2,
+            out_specs=(pl.BlockSpec(memory_space=pltpu.HBM),) * 2,
+            scratch_shapes=[pltpu.SemaphoreType.DMA((2,))],
+        )(
+            pltpu.with_memory_space_constraint(lam, pltpu.VMEM),
+            pltpu.with_memory_space_constraint(grad, pltpu.VMEM),
         )
         return lam, grad.reshape(nodes // groups)
 

time: 41.9 us -> 27.6 us (0.66)
  the two profiles are of different devices: /device:TPU:1 before, /device:TPU:6 now
where the time goes in v3:
time: 27.6 us; the launch traced here: 27.4 us
  Pallas kernels  26.8 us (97%)
  between operations  0.64 us (2%)
    pallas_call x1, Pallas kernels, shards(): pl.pallas_call(functools.partial(kernel, (spaces, groups, pairs, rim, ter...  26.1 us
    pallas_call x1, Pallas kernels, shards(): pl.pallas_call(write_out, out_shape=(pltpu.HBM((sources, nodes), F32), pl...  0.65 us

profile of v3, /device:TPU:6, one launch (start us, length us, event | category | flops | bytes accessed | tf_op | source)
XLA Modules:
  0.0 27.4 jit_solution(3166271937506493715)
XLA Ops:
  0.6 26.1 %shard_map.86 = (f32[8,2048]{1,0:T(8,128)S(1)}, f32[1,128]{1,0:T(1,128)S(1)}) custom-call(f32[8,2048]{1,0:T(8,128)} %misfit_h.1, s32[1,2048]{1,0:T(1,128)} %bitcast.3, bf16[8,2048]{1,0:T(8,128)(2,1)} %field_h.1, bf16[64,2048]{1,0:T(8,128)(2,1)} %diag_h.1, bf16[64,2048]{1,0:T(8,128)(2,1)} %cond_h.1, bf16[6,64,2048]{2,1,0:T(8,128)(2,1)} %off_h.1, s32[6,32]{1,0:T(8,128)} %bitcast.4), custom_call_target="tpu_custom_call" | custom-call | tf_op jit(solution)/shard_map/pallas_call | solution.py:283
  26.8 0.7 %shard_map.87 = (f32[8,2048]{1,0:T(8,128)}, f32[1,128]{1,0:T(1,128)}) custom-call(f32[8,2048]{1,0:T(8,128)S(1)} %get-tuple-element.6.lam, f32[1,128]{1,0:T(1,128)S(1)} %get-tuple-element.7.grad), custom_call_target="tpu_custom_call" | custom-call | tf_op jit(solution)/shard_map/pallas_call | solution.py:326

commit v4 on v3

--- a/solution.py
+++ b/solution.py
@@ -20,7 +20,7 @@
     misfit_v, node_v, field_v, diag_v, cond_v, off_v, index_s,
     rhs_v, driven_v, tiles1, tiles2, tiles_f,
     stage, landed, grad_send, grad_recv,
-    load_sem, halo_send, halo_recv, gsend_sem, grecv_sem,
+    load_sem, halo_send, halo_recv, gsend_sem, grecv_sem, present,
 ):
     spaces, groups, pairs, rim, terms = cfg
     blocks = 2 * pairs
@@ -32,14 +32,14 @@
     loads = []
     for at, (src, dst) in enumerate(
         [
-            (node_h, node_v), (misfit_h, misfit_v), (cond_h, cond_v), (field_h, field_v),
+            (misfit_h, misfit_v), (node_h, node_v), (cond_h, cond_v), (field_h, field_v),
             (index_h, index_s), (diag_h, diag_v), (off_h, off_v),
         ]
     ):
-        copy = pltpu.make_async_copy(src, dst, load_sem.at[at])
+        loads.append(pltpu.make_async_copy(src, dst, load_sem.at[at]))
+    misfit_l, node_l, cond_l, field_l, index_l, diag_l, off_l = loads
+    for copy in loads[:3]:
         copy.start()
-        loads.append(copy)
-    node_l, misfit_l, cond_l, field_l, index_l, diag_l, off_l = loads
 
     me = lax.axis_index("space")
     group = lax.axis_index("src")
@@ -55,9 +55,14 @@
                 barrier, inc=1, device_id={"space": neighbour}, device_id_type=MESH
             )
 
-    for step in range(1, groups):
-        peer = lax.rem(group + step, groups)
+    core = group + 1 - 2 * lax.rem(group, 2)
+    across = group + 2 - 4 * lax.rem(lax.div(group, 2), 2)
+    after = lax.rem(group + 4, groups)
+    before = lax.rem(group + groups - 4, groups)
+    for peer in (after, before, across, core):
         pl.semaphore_signal(barrier, inc=1, device_id={"src": peer}, device_id_type=MESH)
+    for copy in loads[3:]:
+        copy.start()
 
     left = lax.broadcasted_iota(jnp.int32, (8, 128), 1) < 64
     upper_rows = lax.broadcasted_iota(jnp.int32, (16, 128), 0) < 8
@@ -126,15 +131,15 @@
 
     def stage_side(which, side, values):
         for at in range(0, ext, 2):
-            stage[which, side, at // 2] = jnp.concatenate(
+            stage[side, which, at // 2] = jnp.concatenate(
                 [values[at], values[at + 1]], axis=0
             ).astype(BF16)
 
     def halo(which, side):
         return pltpu.make_async_remote_copy(
-            src_ref=stage.at[which, side],
+            src_ref=stage.at[side, which],
             dst_ref=landed.at[which, 1 - side],
-            send_sem=halo_send.at[2 * which + side],
+            send_sem=halo_send.at[side],
             recv_sem=halo_recv.at[2 * which + 1 - side],
             device_id={"space": down if side == 0 else up},
             device_id_type=MESH,
@@ -159,22 +164,27 @@
 
     cond_l.wait()
     lam = [None] * pairs
-    for pair in (*low, *high):
+    for pair in (*high, *low):
         lam[pair] = smooth(pair, rhs[pair])
+    stage_side(0, 1, [lam[p] for p in high])
     stage_side(0, 0, [lam[p] for p in low])
-    stage_side(0, 1, [lam[p] for p in high])
+    pl.semaphore_wait(
+        barrier, 4 + jnp.where(has[0], 1, 0) + jnp.where(has[1], 1, 0)
+    )
+    for side in (1, 0):
+        start(0, side)
     field_l.wait()
     field = [field_v[:, lanes(p)].astype(F32) for p in range(pairs)]
-    stage_side(2, 0, [field[p] for p in low])
-    stage_side(2, 1, [field[p] for p in high])
-
-    pl.semaphore_wait(
-        barrier, groups - 1 + jnp.where(has[0], 1, 0) + jnp.where(has[1], 1, 0)
-    )
-    for which in (0, 2):
-        for side in (0, 1):
-            start(which, side)
-
+    for side, own in ((1, high), (0, low)):
+        stage_side(2, side, [field[p] for p in own])
+        start(2, side)
+
+    def tell(at, peer):
+        pl.semaphore_signal(
+            present.at[at], inc=1, device_id={"src": peer}, device_id_type=MESH
+        )
+
+    tell(0, after)
     for pair in inner:
         lam[pair] = smooth(pair, rhs[pair])
     for pair in range(pairs):
@@ -192,25 +202,30 @@
             lam[pair] = lam[pair] + step
 
     sweep(inner, tiles1)
-    for side, own in ((0, low), (1, high)):
+    for side, own in ((1, high), (0, low)):
         receive(0, side, tiles1)
         sweep(own, tiles1)
         stage_side(1, side, [lam[p] for p in own])
         start(1, side)
+    pl.semaphore_wait(present.at[0], 1)
+    tell(1, across)
     for pair in range(pairs):
         expand(tiles2, rim + 2 * pair, lam[pair])
 
-    for side in (0, 1):
+    for side in (1, 0):
         receive(2, side, tiles_f)
     for pair in range(pairs):
         driven_v[pair] = apply(pair, tiles_f)
+
+    pl.semaphore_wait(present.at[1], 1)
+    tell(2, core)
 
     def send_row(pair):
         return pltpu.make_async_remote_copy(
             src_ref=grad_send.at[pair],
             dst_ref=grad_recv.at[group],
-            send_sem=gsend_sem.at[pair],
-            recv_sem=grecv_sem.at[group],
+            send_sem=gsend_sem.at[0],
+            recv_sem=grecv_sem.at[0],
             device_id={"src": pair},
             device_id_type=MESH,
         )
@@ -227,31 +242,22 @@
             def _():
                 send_row(pair).start()
 
+    pl.semaphore_wait(present.at[2], 1)
     finish(inner)
     for side, own in ((0, low), (1, high)):
         receive(1, side, tiles2)
         finish(own)
 
     grad_recv[pl.ds(group, 1)] = grad_send[pl.ds(group, 1)]
-    for which in range(3):
-        for side in (0, 1):
-
-            @pl.when(has[side])
-            def _():
-                halo(which, side).wait_send()
-
-    for peer in range(groups):
-
-        @pl.when(group != peer)
+    for side in (0, 1):
+
+        @pl.when(has[side])
         def _():
-            pltpu.make_async_remote_copy(
-                src_ref=grad_send.at[peer],
-                dst_ref=grad_recv.at[peer],
-                send_sem=gsend_sem.at[peer],
-                recv_sem=grecv_sem.at[peer],
-                device_id={"src": peer},
-                device_id_type=MESH,
-            ).wait()
+            pltpu.make_async_copy(stage.at[side], stage.at[side], halo_send.at[side]).wait()
+
+    others = pl.ds(0, groups - 1)
+    for sem in (gsend_sem, grecv_sem):
+        pltpu.make_async_copy(grad_send.at[others], grad_recv.at[others], sem.at[0]).wait()
 
     grad_out[...] = jnp.sum(grad_recv[...], axis=0)
 
@@ -301,15 +307,16 @@
                 pltpu.VMEM((ext_blocks, 16, 128), BF16),
                 pltpu.VMEM((ext_blocks, 16, 128), BF16),
                 pltpu.VMEM((ext_blocks, 16, 128), BF16),
-                pltpu.VMEM((3, 2, sent, 16, 128), BF16),
+                pltpu.VMEM((2, 3, sent, 16, 128), BF16),
                 pltpu.VMEM((3, 2, sent, 16, 128), BF16),
                 pltpu.VMEM((pairs, 1, 128), F32),
                 pltpu.VMEM((groups, 1, 128), F32),
                 pltpu.SemaphoreType.DMA((7,)),
+                pltpu.SemaphoreType.DMA((2,)),
                 pltpu.SemaphoreType.DMA((6,)),
-                pltpu.SemaphoreType.DMA((6,)),
-                pltpu.SemaphoreType.DMA((pairs,)),
-                pltpu.SemaphoreType.DMA((groups,)),
+                pltpu.SemaphoreType.DMA((1,)),
+                pltpu.SemaphoreType.DMA((1,)),
+                pltpu.SemaphoreType.REGULAR((3,)),
             ],
             compiler_params=pltpu.CompilerParams(
                 collective_id=0, has_side_effects=True, vmem_limit_bytes=32 * 1024 * 1024

time: 27.6 us -> 26.5 us (0.960)
  Pallas kernels: 26.8 us -> 25.7 us
    pallas_call x1, Pallas kernels: 26.1 us -> 25 us  [shards(): pl.pallas_call(functools.partial(kernel, (spaces, groups, pairs, rim, ter...]
where the time goes in v4:
time: 26.5 us; the launch traced here: 26.3 us
  Pallas kernels  25.7 us (97%)
  between operations  0.64 us (2%)
    pallas_call x1, Pallas kernels, shards(): pl.pallas_call(functools.partial(kernel, (spaces, groups, pairs, rim, ter...  25 us
    pallas_call x1, Pallas kernels, shards(): pl.pallas_call(write_out, out_shape=(pltpu.HBM((sources, nodes), F32), pl...  0.65 us

profile of v4, /device:TPU:6, one launch (start us, length us, event | category | flops | bytes accessed | tf_op | source)
XLA Modules:
  0.0 26.3 jit_solution(11304579051391858767)
XLA Ops:
  0.6 25.0 %shard_map.86 = (f32[8,2048]{1,0:T(8,128)S(1)}, f32[1,128]{1,0:T(1,128)S(1)}) custom-call(f32[8,2048]{1,0:T(8,128)} %misfit_h.1, s32[1,2048]{1,0:T(1,128)} %bitcast.3, bf16[8,2048]{1,0:T(8,128)(2,1)} %field_h.1, bf16[64,2048]{1,0:T(8,128)(2,1)} %diag_h.1, bf16[64,2048]{1,0:T(8,128)(2,1)} %cond_h.1, bf16[6,64,2048]{2,1,0:T(8,128)(2,1)} %off_h.1, s32[6,32]{1,0:T(8,128)} %bitcast.4), custom_call_target="tpu_custom_call" | custom-call | tf_op jit(solution)/shard_map/pallas_call | solution.py:289
  25.7 0.7 %shard_map.87 = (f32[8,2048]{1,0:T(8,128)}, f32[1,128]{1,0:T(1,128)}) custom-call(f32[8,2048]{1,0:T(8,128)S(1)} %get-tuple-element.6.lam, f32[1,128]{1,0:T(1,128)S(1)} %get-tuple-element.7.grad), custom_call_target="tpu_custom_call" | custom-call | tf_op jit(solution)/shard_map/pallas_call | solution.py:333

commit v5 on v4

--- a/solution.py
+++ b/solution.py
@@ -18,7 +18,7 @@
     misfit_h, node_h, field_h, diag_h, cond_h, off_h, index_h,
     lam_out, grad_out,
     misfit_v, node_v, field_v, diag_v, cond_v, off_v, index_s,
-    rhs_v, driven_v, tiles1, tiles2, tiles_f,
+    rhs_v, cond2_v, driven_v, tiles1, tiles2, tiles_f,
     stage, landed, grad_send, grad_recv,
     load_sem, halo_send, halo_recv, gsend_sem, grecv_sem, present,
 ):
@@ -93,16 +93,15 @@
         part = lax.dot_general(spread, hot, NT, preferred_element_type=F32)
         total = part if total is None else total + part
     rhs = [total[16 * p : 16 * p + 8] + total[16 * p + 8 : 16 * p + 16] for p in range(pairs)]
-    for pair in range(pairs):
-        rhs_v[pair] = rhs[pair]
-
-    def join(y):
-        return jnp.concatenate([y[0:8], y[8:16]], axis=1)
+
+    def pick(y):
+        return jnp.where(left, y[0:8], y[8:16])
 
     def smooth(pair, res):
         x = jnp.concatenate([jnp.where(left, res, zero), jnp.where(left, zero, res)], axis=0)
         w = cond_v[:, lanes(pair)]
-        return join(lax.dot_general(x.astype(BF16), w, NT, preferred_element_type=F32))
+        w = jnp.concatenate([w, w], axis=0)
+        return pick(lax.dot_general(x.astype(BF16), w, NT, preferred_element_type=F32))
 
     def expand(tiles, first, v):
         swapped = pltpu.roll(v, 64, 1)
@@ -127,7 +126,7 @@
             weights.append(off_v[k, :, lanes(pair)])
         x = jnp.concatenate(parts, axis=1)
         w = jnp.concatenate(weights, axis=1)
-        return join(lax.dot_general(x, w, NT, preferred_element_type=F32))
+        return lax.dot_general(x, w, NT, preferred_element_type=F32)
 
     def stage_side(which, side, values):
         for at in range(0, ext, 2):
@@ -164,15 +163,15 @@
 
     cond_l.wait()
     lam = [None] * pairs
-    for pair in (*high, *low):
+    for pair in high:
         lam[pair] = smooth(pair, rhs[pair])
     stage_side(0, 1, [lam[p] for p in high])
+    pl.semaphore_wait(barrier, 4 + jnp.where(has[0], 1, 0) + jnp.where(has[1], 1, 0))
+    start(0, 1)
+    for pair in low:
+        lam[pair] = smooth(pair, rhs[pair])
     stage_side(0, 0, [lam[p] for p in low])
-    pl.semaphore_wait(
-        barrier, 4 + jnp.where(has[0], 1, 0) + jnp.where(has[1], 1, 0)
-    )
-    for side in (1, 0):
-        start(0, side)
+    start(0, 0)
     field_l.wait()
     field = [field_v[:, lanes(p)].astype(F32) for p in range(pairs)]
     for side, own in ((1, high), (0, low)):
@@ -191,34 +190,45 @@
         expand(tiles1, rim + 2 * pair, lam[pair])
         expand(tiles_f, rim + 2 * pair, field[pair])
 
+    for pair in range(pairs):
+        rhs_v[pair] = jnp.concatenate([rhs[pair], pltpu.roll(rhs[pair], 64, 1)], axis=0)
+        w = cond_v[:, lanes(pair)]
+        cond2_v[pair] = jnp.concatenate([w[:, 0:64], w[:, 64:128]], axis=0)
+
     index_l.wait()
     diag_l.wait()
     off_l.wait()
 
     def sweep(some, tiles):
         products = [apply(pair, tiles) for pair in some]
-        steps = [smooth(pair, rhs_v[pair] - y) for pair, y in zip(some, products)]
+        residues = [
+            (rhs_v[pair, :, 0:64] - y).astype(BF16) for pair, y in zip(some, products)
+        ]
+        steps = [
+            lax.dot_general(res, cond2_v[pair], NT, preferred_element_type=F32)
+            for pair, res in zip(some, residues)
+        ]
         for pair, step in zip(some, steps):
-            lam[pair] = lam[pair] + step
-
+            lam[pair] = lam[pair] + pick(step)
+
+    pl.semaphore_wait(present.at[0], 1)
+    tell(1, across)
     sweep(inner, tiles1)
+    pl.semaphore_wait(present.at[1], 1)
+    tell(2, core)
     for side, own in ((1, high), (0, low)):
         receive(0, side, tiles1)
         sweep(own, tiles1)
         stage_side(1, side, [lam[p] for p in own])
         start(1, side)
-    pl.semaphore_wait(present.at[0], 1)
-    tell(1, across)
     for pair in range(pairs):
         expand(tiles2, rim + 2 * pair, lam[pair])
 
     for side in (1, 0):
         receive(2, side, tiles_f)
     for pair in range(pairs):
-        driven_v[pair] = apply(pair, tiles_f)
-
-    pl.semaphore_wait(present.at[1], 1)
-    tell(2, core)
+        y = apply(pair, tiles_f)
+        driven_v[pair] = jnp.concatenate([y[0:8], y[8:16]], axis=1)
 
     def send_row(pair):
         return pltpu.make_async_remote_copy(
@@ -302,7 +312,8 @@
                 pltpu.VMEM((width, nodes), BF16),
                 pltpu.VMEM((terms, width, nodes), BF16),
                 pltpu.SMEM((terms, blocks), jnp.int32),
-                pltpu.VMEM((pairs, sources, 128), F32),
+                pltpu.VMEM((pairs, 16, 128), F32),
+                pltpu.VMEM((pairs, 128, width), BF16),
                 pltpu.VMEM((pairs, sources, 128), F32),
                 pltpu.VMEM((ext_blocks, 16, 128), BF16),
                 pltpu.VMEM((ext_blocks, 16, 128), BF16),

time: 26.5 us -> 26.4 us (level)
  no operation moved by 1% of the time
where the time goes in v5:
time: 26.4 us; the launch traced here: 26.3 us
  Pallas kernels  25.6 us (97%)
  between operations  0.64 us (2%)
    pallas_call x1, Pallas kernels, shards(): pl.pallas_call(functools.partial(kernel, (spaces, groups, pairs, rim, ter...  25 us
    pallas_call x1, Pallas kernels, shards(): pl.pallas_call(write_out, out_shape=(pltpu.HBM((sources, nodes), F32), pl...  0.65 us

profile of v5, /device:TPU:6, one launch (start us, length us, event | category | flops | bytes accessed | tf_op | source)
XLA Modules:
  0.0 26.3 jit_solution(16081616090625640860)
XLA Ops:
  0.6 25.0 %shard_map.86 = (f32[8,2048]{1,0:T(8,128)S(1)}, f32[1,128]{1,0:T(1,128)S(1)}) custom-call(f32[8,2048]{1,0:T(8,128)} %misfit_h.1, s32[1,2048]{1,0:T(1,128)} %bitcast.3, bf16[8,2048]{1,0:T(8,128)(2,1)} %field_h.1, bf16[64,2048]{1,0:T(8,128)(2,1)} %diag_h.1, bf16[64,2048]{1,0:T(8,128)(2,1)} %cond_h.1, bf16[6,64,2048]{2,1,0:T(8,128)(2,1)} %off_h.1, s32[6,32]{1,0:T(8,128)} %bitcast.4), custom_call_target="tpu_custom_call" | custom-call | tf_op jit(solution)/shard_map/pallas_call | solution.py:299
  25.6 0.7 %shard_map.87 = (f32[8,2048]{1,0:T(8,128)}, f32[1,128]{1,0:T(1,128)}) custom-call(f32[8,2048]{1,0:T(8,128)S(1)} %get-tuple-element.6.lam, f32[1,128]{1,0:T(1,128)S(1)} %get-tuple-element.7.grad), custom_call_target="tpu_custom_call" | custom-call | tf_op jit(solution)/shard_map/pallas_call | solution.py:344

commit v6 on v5

--- a/solution.py
+++ b/solution.py
@@ -38,8 +38,6 @@
     ):
         loads.append(pltpu.make_async_copy(src, dst, load_sem.at[at]))
     misfit_l, node_l, cond_l, field_l, index_l, diag_l, off_l = loads
-    for copy in loads[:3]:
-        copy.start()
 
     me = lax.axis_index("space")
     group = lax.axis_index("src")
@@ -61,7 +59,7 @@
     before = lax.rem(group + groups - 4, groups)
     for peer in (after, before, across, core):
         pl.semaphore_signal(barrier, inc=1, device_id={"src": peer}, device_id_type=MESH)
-    for copy in loads[3:]:
+    for copy in loads:
         copy.start()
 
     left = lax.broadcasted_iota(jnp.int32, (8, 128), 1) < 64
@@ -168,6 +166,12 @@
     stage_side(0, 1, [lam[p] for p in high])
     pl.semaphore_wait(barrier, 4 + jnp.where(has[0], 1, 0) + jnp.where(has[1], 1, 0))
     start(0, 1)
+    def tell(at, peer):
+        pl.semaphore_signal(
+            present.at[at], inc=1, device_id={"src": peer}, device_id_type=MESH
+        )
+
+    tell(0, after)
     for pair in low:
         lam[pair] = smooth(pair, rhs[pair])
     stage_side(0, 0, [lam[p] for p in low])
@@ -178,12 +182,6 @@
         stage_side(2, side, [field[p] for p in own])
         start(2, side)
 
-    def tell(at, peer):
-        pl.semaphore_signal(
-            present.at[at], inc=1, device_id={"src": peer}, device_id_type=MESH
-        )
-
-    tell(0, after)
     for pair in inner:
         lam[pair] = smooth(pair, rhs[pair])
     for pair in range(pairs):
@@ -240,20 +238,21 @@
             device_id_type=MESH,
         )
 
-    def finish(some):
+    def finish(some, first=False):
         sweep(some, tiles2)
         rows = [-jnp.sum(lam[p] * driven_v[p], axis=0, keepdims=True) for p in some]
         for pair, row in zip(some, rows):
             grad_send[pair] = row
             lam_out[:, lanes(pair)] = lam[pair]
+        if first:
+            pl.semaphore_wait(present.at[2], 1)
         for pair in some:
 
             @pl.when(group != pair)
             def _():
                 send_row(pair).start()
 
-    pl.semaphore_wait(present.at[2], 1)
-    finish(inner)
+    finish(inner, first=True)
     for side, own in ((0, low), (1, high)):
         receive(1, side, tiles2)
         finish(own)

time: 26.4 us -> 26.2 us (level)
  no operation moved by 1% of the time
where the time goes in v6:
time: 26.2 us; the launch traced here: 26.1 us
  Pallas kernels  25.4 us (97%)
  between operations  0.64 us (2%)
    pallas_call x1, Pallas kernels, shards(): pl.pallas_call(functools.partial(kernel, (spaces, groups, pairs, rim, ter...  24.8 us
    pallas_call x1, Pallas kernels, shards(): pl.pallas_call(write_out, out_shape=(pltpu.HBM((sources, nodes), F32), pl...  0.65 us

profile of v6, /device:TPU:6, one launch (start us, length us, event | category | flops | bytes accessed | tf_op | source)
XLA Modules:
  0.0 26.1 jit_solution(3269993757198356737)
XLA Ops:
  0.6 24.8 %shard_map.86 = (f32[8,2048]{1,0:T(8,128)S(1)}, f32[1,128]{1,0:T(1,128)S(1)}) custom-call(f32[8,2048]{1,0:T(8,128)} %misfit_h.1, s32[1,2048]{1,0:T(1,128)} %bitcast.3, bf16[8,2048]{1,0:T(8,128)(2,1)} %field_h.1, bf16[64,2048]{1,0:T(8,128)(2,1)} %diag_h.1, bf16[64,2048]{1,0:T(8,128)(2,1)} %cond_h.1, bf16[6,64,2048]{2,1,0:T(8,128)(2,1)} %off_h.1, s32[6,32]{1,0:T(8,128)} %bitcast.4), custom_call_target="tpu_custom_call" | custom-call | tf_op jit(solution)/shard_map/pallas_call | solution.py:298
  25.4 0.7 %shard_map.87 = (f32[8,2048]{1,0:T(8,128)}, f32[1,128]{1,0:T(1,128)}) custom-call(f32[8,2048]{1,0:T(8,128)S(1)} %get-tuple-element.6.lam, f32[1,128]{1,0:T(1,128)S(1)} %get-tuple-element.7.grad), custom_call_target="tpu_custom_call" | custom-call | tf_op jit(solution)/shard_map/pallas_call | solution.py:343

commit v7 on v6

--- a/solution.py
+++ b/solution.py
@@ -178,9 +178,6 @@
     start(0, 0)
     field_l.wait()
     field = [field_v[:, lanes(p)].astype(F32) for p in range(pairs)]
-    for side, own in ((1, high), (0, low)):
-        stage_side(2, side, [field[p] for p in own])
-        start(2, side)
 
     for pair in inner:
         lam[pair] = smooth(pair, rhs[pair])
@@ -212,6 +209,9 @@
     pl.semaphore_wait(present.at[0], 1)
     tell(1, across)
     sweep(inner, tiles1)
+    for side, own in ((1, high), (0, low)):
+        stage_side(2, side, [field[p] for p in own])
+        start(2, side)
     pl.semaphore_wait(present.at[1], 1)
     tell(2, core)
     for side, own in ((1, high), (0, low)):

time: 26.2 us -> 26.2 us (level)
  no operation moved by 1% of the time
where the time goes in v7:
time: 26.2 us; the launch traced here: 26.1 us
  Pallas kernels  25.4 us (97%)
  between operations  0.64 us (2%)
    pallas_call x1, Pallas kernels, shards(): pl.pallas_call(functools.partial(kernel, (spaces, groups, pairs, rim, ter...  24.8 us
    pallas_call x1, Pallas kernels, shards(): pl.pallas_call(write_out, out_shape=(pltpu.HBM((sources, nodes), F32), pl...  0.65 us

profile of v7, /device:TPU:6, one launch (start us, length us, event | category | flops | bytes accessed | tf_op | source)
XLA Modules:
  0.0 26.1 jit_solution(3870116117632427274)
XLA Ops:
  0.6 24.8 %shard_map.86 = (f32[8,2048]{1,0:T(8,128)S(1)}, f32[1,128]{1,0:T(1,128)S(1)}) custom-call(f32[8,2048]{1,0:T(8,128)} %misfit_h.1, s32[1,2048]{1,0:T(1,128)} %bitcast.3, bf16[8,2048]{1,0:T(8,128)(2,1)} %field_h.1, bf16[64,2048]{1,0:T(8,128)(2,1)} %diag_h.1, bf16[64,2048]{1,0:T(8,128)(2,1)} %cond_h.1, bf16[6,64,2048]{2,1,0:T(8,128)(2,1)} %off_h.1, s32[6,32]{1,0:T(8,128)} %bitcast.4), custom_call_target="tpu_custom_call" | custom-call | tf_op jit(solution)/shard_map/pallas_call | solution.py:298
  25.4 0.7 %shard_map.87 = (f32[8,2048]{1,0:T(8,128)}, f32[1,128]{1,0:T(1,128)}) custom-call(f32[8,2048]{1,0:T(8,128)S(1)} %get-tuple-element.6.lam, f32[1,128]{1,0:T(1,128)S(1)} %get-tuple-element.7.grad), custom_call_target="tpu_custom_call" | custom-call | tf_op jit(solution)/shard_map/pallas_call | solution.py:343
